TPU v7x, 32 devices: a whole 2x2x4 slice. The times are simulated.
32 devices in a mesh: groups: 2 (over y), pool: 4 (over z), tensor: 4 (over x, core).
Axes of the slice: x: 2, y: 2, z: 4, core: 2. Of those that a mesh axis runs over, the one named last changes fastest.
Arguments:
- tokens: bfloat16 [256, 4096], P(('groups', 'pool'), 'tensor'), parts along dimension 0, may hold values from -6 to 6
- route_ids: int32 [256, 8], P(('groups', 'pool')), parts along dimension 0, may hold values from 0 to 63, all different within a row; in each aligned block of 32 rows (0 to 31, 32 to 63, ...) at most 6 rows name the same one
- route_weights: float32 [256, 8], P(('groups', 'pool')), parts along dimension 0, may hold values from 0.03 to 0.6
- gate_weight: bfloat16 [64, 4096, 768], P('pool', None, 'tensor'), may hold values from -0.09375 to 0.09375
- up_weight: bfloat16 [64, 4096, 768], P('pool', None, 'tensor'), may hold values from -0.09375 to 0.09375
- down_weight: bfloat16 [64, 768, 4096], P('pool', 'tensor'), may hold values from -0.21875 to 0.21875
- queries: bfloat16 [32, 4, 16, 128], P(('groups', 'pool'), 'tensor'), parts along dimension 0, may hold values from -160 to 160
- keys: bfloat16 [32, 4, 128, 128], P(('groups', 'pool'), 'tensor'), parts along dimension 0, may hold values from -6 to 6
- values: bfloat16 [32, 4, 128, 128], P(('groups', 'pool'), 'tensor'), parts along dimension 0, may hold values from -6 to 6
- lengths: int32 [32], P(('groups', 'pool')), parts along dimension 0, may hold values from 1 to 128, as said below
Outputs:
- attention: bfloat16 [32, 4, 16, 128], P(('groups', 'pool')), parts along dimension 0
- combined: bfloat16 [256, 4096], P(('groups', 'pool'), 'tensor'), parts along dimension 0
There are 2 independent parts, one for each index of `groups`. A program takes and returns all parts, laid end to end along the dimension named above; an argument that names none is the same for every part. Nothing has to cross between parts.
Inputs may be any that keep to these rules, and one draw needn't show every extreme that they name: `route_ids`: each row names 8 different experts; among the 32 tokens of one index of pool no expert is named more than 6 times, a bound that some block reaches. `lengths`: the first sequence has all 128 positions live.
All inputs are finite; a program needn't handle non-finite values.
Results may differ from a plain program's by a relative error of at most 0.014.
Values may be sent and summed in bfloat16 or wider, within the bound.
A program may use at most 192 MiB of HBM per device.

v0:
```python
import functools

import jax
import jax.numpy as jnp
from jax import lax
from jax.experimental import pallas as pl
from jax.experimental.pallas import tpu as pltpu
from jax.sharding import PartitionSpec as P

CAP = 6
TILE = 256
SPARE = 2
F32 = jnp.float32
BF16 = jnp.bfloat16
VMEM_LIMIT = 60 * 1024 * 1024


def attend(queries, keys, values, lengths):
    scale = queries.shape[-1] ** (-0.5)
    scores = (
        jnp.einsum("sjgh,sjch->sjgc", queries, keys, preferred_element_type=jnp.float32) * scale
    )
    position = lax.broadcasted_iota(jnp.int32, (keys.shape[0], keys.shape[2]), 1)
    live = position < lengths[:, None]
    scores = jnp.where(live[:, None, None, :], scores, -1e30)
    highest = jnp.max(scores, axis=3, keepdims=True)
    probs = jnp.exp(scores - highest)
    weights = (probs / jnp.sum(probs, axis=3, keepdims=True)).astype(jnp.bfloat16)
    mixed = jnp.einsum("sjgc,sjch->sjgh", weights, values, preferred_element_type=jnp.float32)
    return mixed.astype(jnp.bfloat16)


def slot_table(route_ids, experts, capacity):
    flat_ids = route_ids.reshape(-1)
    count = flat_ids.shape[0]
    onehot = (flat_ids[:, None] == lax.broadcasted_iota(jnp.int32, (1, experts), 1)).astype(
        jnp.int32
    )
    before = jnp.cumsum(onehot, axis=0) - onehot
    rank = jnp.sum(before * onehot, axis=1)
    slot = flat_ids * capacity + rank
    owner = lax.broadcasted_iota(jnp.int32, (count,), 0) // route_ids.shape[1]
    source = jnp.full((experts * capacity,), -1, jnp.int32).at[slot].set(owner)
    return (slot, source)


def routed_shards(
    tokens, route_ids, route_weights, gate_weight, up_weight, down_weight,
    queries, keys, values, lengths,
):
    local_heads = attend(queries, keys, values, lengths)
    attention = lax.all_gather(local_heads, "tensor", axis=1, tiled=True)
    pool_size = lax.axis_size("pool")
    local_experts = gate_weight.shape[0]
    experts = local_experts * pool_size
    slot, source = slot_table(route_ids, experts, CAP)
    filled = (source >= 0)[:, None]
    picked = jnp.maximum(source, 0)
    whole = lax.all_gather(tokens, "tensor", axis=1, tiled=True)
    outgoing = jnp.where(filled, whole[picked], jnp.zeros((), whole.dtype))
    outgoing = outgoing.reshape(pool_size, local_experts, CAP, whole.shape[1])
    arrived = lax.all_to_all(outgoing, "pool", split_axis=0, concat_axis=0, tiled=True)
    gate = jnp.einsum("pech,ehf->pecf", arrived, gate_weight, preferred_element_type=jnp.float32)
    up = jnp.einsum("pech,ehf->pecf", arrived, up_weight, preferred_element_type=jnp.float32)
    hidden = (jax.nn.silu(gate) * up).astype(jnp.bfloat16)
    partial_value = jnp.einsum(
        "pecf,efd->pecd", hidden, down_weight, preferred_element_type=jnp.float32
    )
    summed = lax.psum_scatter(
        partial_value.astype(jnp.bfloat16), "tensor", scatter_dimension=3, tiled=True
    )
    returned = lax.all_to_all(summed, "pool", split_axis=0, concat_axis=0, tiled=True)
    fetched = returned.reshape(experts * CAP, returned.shape[3])[slot]
    fetched = fetched.reshape(route_ids.shape[0], route_ids.shape[1], returned.shape[3])
    combined = jnp.sum(fetched.astype(jnp.float32) * route_weights[:, :, None], axis=1)
    return (attention, combined.astype(jnp.bfloat16))


def kernel(
    experts, len_ref, tok_hbm, ids_ref, rw_ref, q_hbm, k_hbm, v_hbm, gate_hbm, up_hbm, down_hbm,
    attn_ref, comb_ref,
    x, tab_out, tab_in, table, q_buf, k_buf, v_buf, heads_own, heads_in, ring, hid, acc,
    c1_out, c1_in, x_out, x_in, c3_out, c3_in, z_out, z_in,
    w_sem, l_sem, s_sem, r_sem,
):
    pools, rows, width = x.shape[1:]
    toks = pools * rows
    units = gate_hbm.shape[0]
    ff = units // experts
    tiles = units // TILE
    slots = ring.shape[0]
    spare = slots - 2 * tiles
    p = lax.axis_index("pool")
    t = lax.axis_index("tensor")
    core = t + 1 - 2 * (t % 2)
    across = (t + 2) % 4
    corner = (core + 2) % 4
    blocks = (corner, across, core, t)
    near = [j for j in (1, 3, 2) if j < pools]
    far = [j for j in (2, 1, 3) if j < pools]

    barrier = pltpu.get_barrier_semaphore()
    for j in range(1, pools):
        pl.semaphore_signal(barrier, inc=1, device_id={"pool": (p + j) % pools})
    for j in range(1, 4):
        pl.semaphore_signal(barrier, inc=1, device_id={"tensor": (t + j) % 4})

    def weight(src, i, slot):
        at = pl.ds(pl.multiple_of(i * TILE, TILE), TILE)
        return pltpu.make_async_copy(src.at[at], ring.at[slot], w_sem.at[slot])

    own = pltpu.make_async_copy(tok_hbm, x.at[t, p], l_sem.at[0])
    own.start()
    for i in range(tiles):
        weight(gate_hbm, i, 2 * i).start()
        weight(up_hbm, i, 2 * i + 1).start()
        if i == 1:
            pl.semaphore_wait(barrier, pools + 2)
            count = [0]
            sent = []

            def send(src, dst, where):
                n = count[0]
                count[0] = n + 1
                copy = pltpu.make_async_remote_copy(
                    src_ref=src, dst_ref=dst, send_sem=s_sem.at[n], recv_sem=r_sem.at[n],
                    device_id=where,
                )
                copy.start()
                sent.append(copy)
                return copy

            mine = x.at[t, p]
            z_copies = {}
            for j in far:
                z_copies[j] = send(tok_hbm, mine, {"pool": (p + pools - j) % pools})
            x_copies = [send(tok_hbm, mine, {"tensor": across})]
            core_copies = [send(tok_hbm, mine, {"tensor": core})]
    for i in range(spare):
        weight(down_hbm, i, 2 * tiles + i).start()
    loads = [
        pltpu.make_async_copy(src, dst, l_sem.at[n + 1])
        for n, (src, dst) in enumerate(((q_hbm, q_buf), (k_hbm, k_buf), (v_hbm, v_buf)))
    ]
    for copy in loads:
        copy.start()

    expert = lax.broadcasted_iota(jnp.int32, (experts, rows), 0)
    tab_copies = []
    for j in far + [0]:
        owner = (p + pools - j) % pools
        total = jnp.zeros((experts, rows), F32)
        for k in range(ids_ref.shape[0]):
            hit = (ids_ref[k : k + 1, :] - owner * experts) == expert
            total = total + jnp.where(hit, rw_ref[k : k + 1, :], 0.0)
        if j == 0:
            tab_in[p] = total
        else:
            tab_out[j] = total
            tab_copies.append(send(tab_out.at[j], tab_in.at[p], {"pool": owner}))

    for j in near:
        z_copies[j].wait_recv()
        block = x.at[t, (p + j) % pools]
        x_copies.append(send(block, block, {"tensor": across}))
        core_copies.append(send(block, block, {"tensor": core}))
    for n, j in enumerate([0] + near):
        x_copies[n].wait_recv()
        block = x.at[across, (p + j) % pools]
        core_copies.append(send(block, block, {"tensor": core}))
    for copy in tab_copies:
        copy.wait_recv()
    table[...] = jnp.concatenate([tab_in[n] for n in range(pools)], axis=1)
    own.wait()
    for copy in core_copies:
        copy.wait_recv()

    unit = lax.broadcasted_iota(jnp.int32, (TILE, toks), 0)
    dims = (((1,), (1,)), ((), ()))

    def step(i, carry):
        weight(gate_hbm, i, 2 * i).wait()
        weight(up_hbm, i, 2 * i + 1).wait()
        gate = jnp.zeros((TILE, toks), F32)
        up = jnp.zeros((TILE, toks), F32)
        for b in range(4):
            xb = x[b].reshape(toks, width)
            at = slice(b * width, (b + 1) * width)
            gate = gate + lax.dot_general(
                ring[2 * i, :, at], xb, dims, preferred_element_type=F32
            )
            up = up + lax.dot_general(
                ring[2 * i + 1, :, at], xb, dims, preferred_element_type=F32
            )
        first = (i * TILE) // ff
        share = jnp.zeros((TILE, toks), F32)
        for m in range((TILE - 2) // ff + 2):
            e = first + m
            row = table[pl.ds(jnp.minimum(e, experts - 1), 1), :]
            inside = (unit >= e * ff - i * TILE) & (unit < (e + 1) * ff - i * TILE)
            share = jnp.where(inside, row, share)
        value = gate / (1.0 + jnp.exp(-gate)) * up * share
        hid[:, pl.ds(pl.multiple_of(i * TILE, TILE), TILE)] = value.T.astype(BF16)

        for m in range(2):

            @pl.when(spare + 2 * i + m < tiles)
            def _():
                weight(down_hbm, spare + 2 * i + m, 2 * i + m).start()

        return carry

    lax.fori_loop(0, tiles, step, 0)

    places = [2 * tiles + j if j < spare else j - spare for j in range(tiles)]
    for j in range(tiles):
        weight(down_hbm, j, places[j]).wait()

    def project(n, dst):
        def column(i, carry):
            at = pl.ds(pl.multiple_of(blocks[n] * width + i * TILE, TILE), TILE)
            out = jnp.zeros((toks, TILE), F32)
            for j in range(tiles):
                out = out + jnp.dot(
                    hid[:, j * TILE : (j + 1) * TILE], ring[places[j], :, at],
                    preferred_element_type=F32,
                )
            dst[:, pl.ds(pl.multiple_of(i * TILE, TILE), TILE)] = out.astype(dst.dtype)
            return carry

        lax.fori_loop(0, width // TILE, column, 0)

    def rows_of(ref, q):
        return ref.at[pl.ds(pl.multiple_of(q * rows, rows), rows)]

    project(0, c1_out)
    first_copy = send(c1_out, c1_in, {"tensor": core})
    project(1, acc)
    first_copy.wait_recv()
    back = {}
    for j in far + [0]:
        q = (p + j) % pools
        piece = rows_of(acc, q)[...] + rows_of(c1_in, q)[...].astype(F32)
        rows_of(x_out, q)[...] = piece.astype(BF16)
        back[j] = send(rows_of(x_out, q), rows_of(x_in, q), {"tensor": across})
    project(2, c3_out)
    third_copy = send(c3_out, c3_in, {"tensor": core})
    project(3, acc)

    for copy in loads:
        copy.wait()
    scale = q_buf.shape[-1] ** (-0.5)
    for s in range(q_buf.shape[0]):
        scores = lax.dot_general(q_buf[s], k_buf[s], dims, preferred_element_type=F32) * scale
        position = lax.broadcasted_iota(jnp.int32, scores.shape, 1)
        scores = jnp.where(position < len_ref[s], scores, -1e30)
        probs = jnp.exp(scores - jnp.max(scores, axis=1, keepdims=True))
        mix = (probs / jnp.sum(probs, axis=1, keepdims=True)).astype(BF16)
        heads_own[s] = jnp.dot(mix, v_buf[s], preferred_element_type=F32).astype(BF16)
    heads_in[t] = heads_own[...]
    head_copies = [
        send(heads_own, heads_in.at[t], {"tensor": (t + j) % 4}) for j in range(1, 4)
    ]

    third_copy.wait_recv()
    last = []
    for j in far + [0]:
        q = (p + j) % pools
        back[j].wait_recv()
        piece = (
            rows_of(acc, q)[...]
            + rows_of(c3_in, q)[...].astype(F32)
            + rows_of(x_in, q)[...].astype(F32)
        )
        if j == 0:
            total = piece
        else:
            z_out[j] = piece.astype(BF16)
            last.append(send(z_out.at[j], z_in.at[j], {"pool": q}))
    for copy in head_copies:
        copy.wait_recv()
    for h in range(4):
        attn_ref[:, h] = heads_in[h]
    for copy in last:
        copy.wait_recv()
    for j in range(1, pools):
        total = total + z_in[j].astype(F32)
    comb_ref[...] = total.astype(BF16)
    for copy in sent:
        copy.wait_send()


def fused_shards(
    tokens, route_ids, route_weights, gate_weight, up_weight, down_weight,
    queries, keys, values, lengths,
):
    pools = lax.axis_size("pool")
    experts, model, ff = gate_weight.shape
    rows, width = tokens.shape
    units = experts * ff
    toks = pools * rows
    seqs, _, group, size = queries.shape
    ctx = keys.shape[2]
    gate_rows = jnp.swapaxes(gate_weight, 1, 2).reshape(units, model)
    up_rows = jnp.swapaxes(up_weight, 1, 2).reshape(units, model)
    down_rows = down_weight.reshape(units, model)
    copies = 3 * pools + 2 * (pools - 1) + 3 + 2 + pools + pools
    vmem = pl.BlockSpec(memory_space=pltpu.VMEM)
    hbm = pl.BlockSpec(memory_space=pl.ANY)
    part = pltpu.VMEM((toks, width), BF16)
    return pl.pallas_call(
        functools.partial(kernel, experts),
        out_shape=(
            jax.ShapeDtypeStruct((seqs, 4, group, size), BF16),
            jax.ShapeDtypeStruct((rows, width), BF16),
        ),
        in_specs=[pl.BlockSpec(memory_space=pltpu.SMEM), hbm, vmem, vmem] + [hbm] * 6,
        out_specs=(vmem, vmem),
        scratch_shapes=[
            pltpu.VMEM((4, pools, rows, width), BF16),
            pltpu.VMEM((pools, experts, rows), F32),
            pltpu.VMEM((pools, experts, rows), F32),
            pltpu.VMEM((experts, toks), F32),
            pltpu.VMEM((seqs, group, size), BF16),
            pltpu.VMEM((seqs, ctx, size), BF16),
            pltpu.VMEM((seqs, ctx, size), BF16),
            pltpu.VMEM((seqs, group, size), BF16),
            pltpu.VMEM((4, seqs, group, size), BF16),
            pltpu.VMEM((2 * (units // TILE) + SPARE, TILE, model), BF16),
            pltpu.VMEM((toks, units), BF16),
            pltpu.VMEM((toks, width), F32),
            part, part, part, part, part, part,
            pltpu.VMEM((pools, rows, width), BF16),
            pltpu.VMEM((pools, rows, width), BF16),
            pltpu.SemaphoreType.DMA((2 * (units // TILE) + SPARE,)),
            pltpu.SemaphoreType.DMA((4,)),
            pltpu.SemaphoreType.DMA((copies,)),
            pltpu.SemaphoreType.DMA((copies,)),
        ],
        compiler_params=pltpu.CompilerParams(
            collective_id=0, has_side_effects=True, vmem_limit_bytes=VMEM_LIMIT
        ),
        cost_estimate=pl.CostEstimate(
            flops=6 * toks * units * model,
            bytes_accessed=6 * units * model,
            transcendentals=toks * units,
        ),
    )(
        lengths, tokens, route_ids.T, route_weights.T,
        queries.reshape(seqs, group, size),
        keys.reshape(seqs, ctx, size),
        values.reshape(seqs, ctx, size),
        gate_rows, up_rows, down_rows,
    )


def solution(mesh):
    in_specs = (
        P(("groups", "pool"), "tensor"),
        P(("groups", "pool"), None),
        P(("groups", "pool"), None),
        P("pool", None, "tensor"),
        P("pool", None, "tensor"),
        P("pool", "tensor", None),
        P(("groups", "pool"), "tensor", None, None),
        P(("groups", "pool"), "tensor", None, None),
        P(("groups", "pool"), "tensor", None, None),
        P(("groups", "pool")),
    )
    out_specs = (P(("groups", "pool"), None, None, None), P(("groups", "pool"), "tensor"))
    fused = mesh.shape["tensor"] == 4 and mesh.shape["pool"] == 4
    shards = fused_shards if fused else routed_shards
    return jax.shard_map(shards, mesh=mesh, in_specs=in_specs, out_specs=out_specs, check_vma=False)
```

profile of v0, /device:TPU:0, one launch (start us, length us, event | category | flops | bytes accessed | tf_op | source)
XLA Modules:
  0.0 55.8 jit_solution(7731009139494056687)
XLA Ops:
  0.6 52.2 %shard_map.113 = (bf16[4,4,16,128]{3,2,1,0:T(8,128)(2,1)}, bf16[32,1024]{1,0:T(8,128)(2,1)}) custom-call(s32[4]{0:T(128)} %len_ref.1, bf16[32,1024]{1,0:T(8,128)(2,1)} %tok_hbm.1, s32[8,32]{1,0:T(8,128)} %bitcast.18, f32[8,32]{1,0:T(8,128)} %bitcast.19, bf16[4,16,128]{2,1,0:T(8,128)(2,1)} %bitcast.17, bf16[4,128,128]{2,1,0:T(8,128)(2,1)} %bitcast.15, ...), custom_call_target="tpu_custom_call" | custom-call | flops 9663676416 | bytes 75497472 | tf_op jit(solution)/shard_map/pallas_call | solution.py:311
  52.9 1.5 %copy.14 = bf16[4,4,16,128]{3,2,1,0:T(8,128)(2,1)} copy(bf16[4,4,16,128]{3,2,1,0:T(8,128)(2,1)} %get-tuple-element.4) | data formatting | bytes 131072
  54.3 1.5 %copy.15 = bf16[32,1024]{1,0:T(8,128)(2,1)} copy(bf16[32,1024]{1,0:T(8,128)(2,1)} %get-tuple-element.5) | data formatting | bytes 131072
where the time goes:
time: 56.1 us; the launch traced here: 55.8 us
  Pallas kernels  52.2 us (93%)
  local copies, waits for them, and re-layouts  2.95 us (5%)
  between operations  0.64 us (1%)
    pallas_call x1, Pallas kernels, fused_shards(): pl.pallas_call(functools.partial(kernel, experts), out_shape=(jax.ShapeDt...  52.2 us
    unnamed x2, local copies, waits for them, and re-layouts  2.95 us

commit v1 on v0

--- a/solution.py
+++ b/solution.py
@@ -10,6 +10,8 @@
 CAP = 6
 TILE = 256
 SPARE = 2
+PAIR = 2
+WIDE = 512
 F32 = jnp.float32
 BF16 = jnp.bfloat16
 VMEM_LIMIT = 60 * 1024 * 1024
@@ -178,9 +180,7 @@
     unit = lax.broadcasted_iota(jnp.int32, (TILE, toks), 0)
     dims = (((1,), (1,)), ((), ()))
 
-    def step(i, carry):
-        weight(gate_hbm, i, 2 * i).wait()
-        weight(up_hbm, i, 2 * i + 1).wait()
+    def tile(i):
         gate = jnp.zeros((TILE, toks), F32)
         up = jnp.zeros((TILE, toks), F32)
         for b in range(4):
@@ -200,17 +200,25 @@
             inside = (unit >= e * ff - i * TILE) & (unit < (e + 1) * ff - i * TILE)
             share = jnp.where(inside, row, share)
         value = gate / (1.0 + jnp.exp(-gate)) * up * share
-        hid[:, pl.ds(pl.multiple_of(i * TILE, TILE), TILE)] = value.T.astype(BF16)
-
-        for m in range(2):
-
-            @pl.when(spare + 2 * i + m < tiles)
+        return value.T.astype(BF16)
+
+    def step(n, carry):
+        for m in range(PAIR):
+            weight(gate_hbm, PAIR * n + m, 2 * (PAIR * n + m)).wait()
+            weight(up_hbm, PAIR * n + m, 2 * (PAIR * n + m) + 1).wait()
+        values = [tile(PAIR * n + m) for m in range(PAIR)]
+        for m in range(PAIR):
+            at = pl.multiple_of((PAIR * n + m) * TILE, TILE)
+            hid[:, pl.ds(at, TILE)] = values[m]
+        for m in range(2 * PAIR):
+
+            @pl.when(spare + 2 * PAIR * n + m < tiles)
             def _():
-                weight(down_hbm, spare + 2 * i + m, 2 * i + m).start()
+                weight(down_hbm, spare + 2 * PAIR * n + m, 2 * PAIR * n + m).start()
 
         return carry
 
-    lax.fori_loop(0, tiles, step, 0)
+    lax.fori_loop(0, tiles // PAIR, step, 0)
 
     places = [2 * tiles + j if j < spare else j - spare for j in range(tiles)]
     for j in range(tiles):
@@ -218,17 +226,17 @@
 
     def project(n, dst):
         def column(i, carry):
-            at = pl.ds(pl.multiple_of(blocks[n] * width + i * TILE, TILE), TILE)
-            out = jnp.zeros((toks, TILE), F32)
+            at = pl.ds(pl.multiple_of(blocks[n] * width + i * WIDE, WIDE), WIDE)
+            out = jnp.zeros((toks, WIDE), F32)
             for j in range(tiles):
                 out = out + jnp.dot(
                     hid[:, j * TILE : (j + 1) * TILE], ring[places[j], :, at],
                     preferred_element_type=F32,
                 )
-            dst[:, pl.ds(pl.multiple_of(i * TILE, TILE), TILE)] = out.astype(dst.dtype)
+            dst[:, pl.ds(pl.multiple_of(i * WIDE, WIDE), WIDE)] = out.astype(dst.dtype)
             return carry
 
-        lax.fori_loop(0, width // TILE, column, 0)
+        lax.fori_loop(0, width // WIDE, column, 0)
 
     def rows_of(ref, q):
         return ref.at[pl.ds(pl.multiple_of(q * rows, rows), rows)]

time: 56.1 us -> 53 us (0.945)
  Pallas kernels: 52.2 us -> 49.2 us
    pallas_call x1, Pallas kernels: 52.2 us -> 49.2 us  [fused_shards(): pl.pallas_call(functools.partial(kernel, experts), out_shape=(jax.ShapeDt...]
where the time goes in v1:
time: 53 us; the launch traced here: 52.8 us
  Pallas kernels  49.2 us (93%)
  local copies, waits for them, and re-layouts  2.95 us (6%)
  between operations  0.64 us (1%)
    pallas_call x1, Pallas kernels, fused_shards(): pl.pallas_call(functools.partial(kernel, experts), out_shape=(jax.ShapeDt...  49.2 us
    unnamed x2, local copies, waits for them, and re-layouts  2.95 us

profile of v1, /device:TPU:0, one launch (start us, length us, event | category | flops | bytes accessed | tf_op | source)
XLA Modules:
  0.0 52.8 jit_solution(6955661769588866247)
XLA Ops:
  0.6 49.2 %shard_map.113 = (bf16[4,4,16,128]{3,2,1,0:T(8,128)(2,1)}, bf16[32,1024]{1,0:T(8,128)(2,1)}) custom-call(s32[4]{0:T(128)} %len_ref.1, bf16[32,1024]{1,0:T(8,128)(2,1)} %tok_hbm.1, s32[8,32]{1,0:T(8,128)} %bitcast.18, f32[8,32]{1,0:T(8,128)} %bitcast.19, bf16[4,16,128]{2,1,0:T(8,128)(2,1)} %bitcast.17, bf16[4,128,128]{2,1,0:T(8,128)(2,1)} %bitcast.15, ...), custom_call_target="tpu_custom_call" | custom-call | flops 9663676416 | bytes 75497472 | tf_op jit(solution)/shard_map/pallas_call | solution.py:319
  49.8 1.5 %copy.14 = bf16[4,4,16,128]{3,2,1,0:T(8,128)(2,1)} copy(bf16[4,4,16,128]{3,2,1,0:T(8,128)(2,1)} %get-tuple-element.4) | data formatting | bytes 131072
  51.3 1.5 %copy.15 = bf16[32,1024]{1,0:T(8,128)(2,1)} copy(bf16[32,1024]{1,0:T(8,128)(2,1)} %get-tuple-element.5) | data formatting | bytes 131072
